TPU v7x, 512 devices: a whole 4x8x8 slice. The times are simulated.
512 devices in a mesh: sec: 8 (over x, core), own: 32 (over y_hi, z), tile: 2 (over y_lo).
Axes of the slice: x: 4, y: 8 (y_hi: 4, y_lo: 2; y = y_hi * 2 + y_lo), z: 8, core: 2. Of those that a mesh axis runs over, the one named last changes fastest.
Arguments:
- couple: bfloat16 [4096, 3, 256, 256], P(('sec', 'own', 'tile')), may hold values from -1.5 to 1.5
- factors: bfloat16 [4096, 256, 256], P(('sec', 'own', 'tile')), as said below
- top_reflect: bfloat16 [4096, 64, 64], P(('sec', 'own', 'tile')), as said below
- wy_factor: bfloat16 [4096, 256, 64], P(('sec', 'own', 'tile')), may hold values from -0.375 to 0.375
- neighbour_ids: int32 [4096, 3], P(('sec', 'own', 'tile')), may hold values from 0 to 4095, as said below
- kept_rank: int32 [4096], P(('sec', 'own', 'tile')), may hold values from 8 to 64, as said below
- merge_map: int32 [4096, 3], P(('sec', 'own', 'tile')), may hold values from 0 to 31, all different within a row; in each aligned block of 8 rows (0 to 7, 8 to 15, ...) at most 2 rows name the same one
Outputs:
- merged: bfloat16 [8, 32, 64, 256], P('sec', 'own', None, 'tile')
Inputs may be any that keep to these rules, and one draw needn't show every extreme that they name: factors[c] is lower triangular with a positive diagonal. top_reflect[c] is lower triangular with a unit diagonal. neighbour_ids[c, j] lies on the device with c's sec and tile index whose own index is one lower (j % 3 == 0) or one higher (j % 3 == 1) than c's, or on the device with c's own and tile index whose sec index is one away (j % 3 == 2); where the first choice leaves the axis, the other side is taken; both ends of the range are reached in every draw. `kept_rank`: a multiple of 8; on every device at least one cluster keeps 64 rows. `merge_map`: a cluster's 3 blocks go to different merged blocks; at most 2 blocks of one device go to one merged block, and some device sends exactly 2 to one.
All inputs are finite; a program needn't handle non-finite values.
Results may differ from a plain program's by a relative error of at most 0.01.
Values may be sent and summed in bfloat16 or wider, within the bound.
A program may use at most 64 MiB of HBM per device.

v0:
```python
import jax
import jax.numpy as jnp
from jax import lax
from jax.sharding import PartitionSpec as P


def padded(array, sides, width):
    for axis, dim in sides:
        count, length = (lax.axis_size(axis), array.shape[dim])
        up = [(i, (i + 1) % count) for i in range(count - 1)]
        down = [(j, i) for i, j in up]
        last = lax.slice_in_dim(array, length - width, length, axis=dim)
        initial = lax.slice_in_dim(array, 0, width, axis=dim)
        before = lax.ppermute(last, axis, up)
        after = lax.ppermute(initial, axis, down)
        array = jnp.concatenate([before, array, after], axis=dim)
    return array


def on_device(couple, factors, top_reflect, wy_factor, neighbour_ids, kept_rank, merge_map):
    clusters, neighbours, block_width, _ = couple.shape
    kept_rows = top_reflect.shape[1]
    owners = lax.axis_size("own")
    tile_count = lax.axis_size("tile")
    half_width = block_width // tile_count
    window = padded(factors.reshape((1, 1) + factors.shape), (("sec", 0), ("own", 1)), 1)
    window = window.reshape(9 * clusters, block_width, block_width)
    device = neighbour_ids // clusters
    own_pos = device // tile_count % owners
    sec_pos = device // (tile_count * owners)
    step_sec = sec_pos - lax.axis_index("sec") + 1
    step_own = own_pos - lax.axis_index("own") + 1
    local_index = (step_sec * 3 + step_own) * clusters + neighbour_ids % clusters
    near_factors = jnp.take(window, local_index, axis=0)
    left = jnp.einsum("cik,cjkl->cjil", factors, couple, preferred_element_type=jnp.float32).astype(
        jnp.bfloat16
    )
    scaled = jnp.einsum(
        "cjil,cjml->cjim", left, near_factors, preferred_element_type=jnp.float32
    ).astype(jnp.bfloat16)
    projected = jnp.einsum(
        "cia,cjim->cjam", wy_factor, scaled, preferred_element_type=jnp.float32
    ).astype(jnp.bfloat16)
    coarse = scaled[:, :, :kept_rows, :].astype(jnp.float32) - jnp.einsum(
        "cab,cjbm->cjam", top_reflect, projected, preferred_element_type=jnp.float32
    )
    live = jnp.arange(kept_rows, dtype=jnp.int32)[None, :] < kept_rank[:, None]
    coarse = jnp.where(live[:, None, :, None], coarse, 0.0).astype(jnp.bfloat16)
    blocks = clusters * neighbours
    capacity = max(2, -(-blocks // owners))
    panels = coarse.reshape(blocks, kept_rows, tile_count, half_width)
    target = merge_map.reshape(blocks)
    owner_ids = jnp.arange(owners, dtype=jnp.int32)
    onehot = (target[:, None] == owner_ids[None, :]).astype(jnp.int32)
    slot_index = jnp.sum((jnp.cumsum(onehot, axis=0) - onehot) * onehot, axis=1)
    placement = (
        (target[None, None, :] == owner_ids[:, None, None])
        & (slot_index[None, None, :] == jnp.arange(capacity, dtype=jnp.int32)[None, :, None])
    ).astype(jnp.bfloat16)
    send_slots = jnp.einsum(
        "dsb,bkhw->dhskw", placement, panels, preferred_element_type=jnp.float32
    ).astype(jnp.bfloat16)
    send_slots = send_slots.reshape(owners * tile_count, capacity, kept_rows, half_width)
    arrived = lax.all_to_all(send_slots, ("own", "tile"), split_axis=0, concat_axis=0, tiled=True)
    merged = jnp.sum(arrived, axis=(0, 1), dtype=jnp.float32)
    return merged.astype(jnp.bfloat16).reshape(1, 1, kept_rows, half_width)


def solution(mesh):
    in_specs = (
        P(("sec", "own", "tile"), None, None, None),
        P(("sec", "own", "tile"), None, None),
        P(("sec", "own", "tile"), None, None),
        P(("sec", "own", "tile"), None, None),
        P(("sec", "own", "tile"), None),
        P(("sec", "own", "tile")),
        P(("sec", "own", "tile"), None),
    )
    out_specs = P("sec", "own", None, "tile")
    return jax.shard_map(
        on_device, mesh=mesh, in_specs=in_specs, out_specs=out_specs, check_vma=False
    )
```

profile of v0, /device:TPU:68, one launch (start us, length us, event | category | flops | bytes accessed | tf_op | source)
XLA Modules:
  0.0 268.3 jit_solution(17086152470540098980)
XLA Ops:
  0.0 0.0 copy-start
  0.0 0.0 copy-start.7
  0.0 2.2 collective-permute-start
  2.2 3.6 %collective-permute-start.1 = (bf16[1,1,8,256,256]{4,3,2,1,0:T(8,128)(2,1)}, bf16[1,1,8,256,256]{4,3,2,1,0:T(8,128)(2,1)S(1)}, u32[]{:S(2)}, u32[]{:S(2)}) collective-permute-start(bf16[1,1,8,256,256]{4,3,2,1,0:T(8,128)(2,1)} %bitcast.47), channel_id=1, source_target_pairs={{64,0},{128,64},{192,128},{256,192},{320,256},{384,320},{448,384},... | collective-permute-start | bytes 3145736 | tf_op jit(solution)/shard_map/ppermute | solution.py:15
  5.9 10.7 %collective-permute-done = bf16[1,1,8,256,256]{4,3,2,1,0:T(8,128)(2,1)S(1)} collective-permute-done((bf16[1,1,8,256,256]{4,3,2,1,0:T(8,128)(2,1)}, bf16[1,1,8,256,256]{4,3,2,1,0:T(8,128)(2,1)S(1)}, u32[]{:S(2)}, u32[]{:S(2)}) %collective-permute-start) | collective-permute-done | bytes 1048608 | tf_op jit(solution)/shard_map/ppermute | solution.py:14
  16.6 1.9 collective-permute-done.1
  18.5 3.6 %pad_maximum_fusion.1 = bf16[3,1,8,256,256]{4,3,2,1,0:T(8,128)(2,1)} fusion(bf16[1,1,8,256,256]{4,3,2,1,0:T(8,128)(2,1)S(1)} %collective-permute-done.1, bf16[1,1,8,256,256]{4,3,2,1,0:T(8,128)(2,1)} %bitcast.48, bf16[1,1,8,256,256]{4,3,2,1,0:T(8,128)(2,1)S(1)} %collective-permute-done), kind=kLoop, calls=%fused_computation.2 | loop fusion | flops 3145728 | bytes 6291456 | tf_op jit(solution)/shard_map/concatenate | solution.py:16
  22.1 0.0 copy-done.1
  22.1 0.0 copy-done.2
  22.1 4.3 %collective-permute-start.2 = (bf16[3,1,8,256,256]{4,3,2,1,0:T(8,128)(2,1)}, bf16[3,1,8,256,256]{4,3,2,1,0:T(8,128)(2,1)}, u32[]{:S(2)}, u32[]{:S(2)}) collective-permute-start(bf16[3,1,8,256,256]{4,3,2,1,0:T(8,128)(2,1)} %pad_maximum_fusion.1), channel_id=1, source_target_pairs={{0,2},{2,4},{4,6},{6,8},{8,10},{10,12},{12,14},{14,16},{16,18},{18... | collective-permute-start | bytes 9437192 | tf_op jit(solution)/shard_map/ppermute | solution.py:14
  26.3 3.2 %collective-permute-start.3 = (bf16[3,1,8,256,256]{4,3,2,1,0:T(8,128)(2,1)}, bf16[3,1,8,256,256]{4,3,2,1,0:T(8,128)(2,1)}, u32[]{:S(2)}, u32[]{:S(2)}) collective-permute-start(bf16[3,1,8,256,256]{4,3,2,1,0:T(8,128)(2,1)} %pad_maximum_fusion.1), channel_id=1, source_target_pairs={{2,0},{4,2},{6,4},{8,6},{10,8},{12,10},{14,12},{16,14},{18,16},{20... | collective-permute-start | bytes 9437192 | tf_op jit(solution)/shard_map/ppermute | solution.py:15
  29.6 0.1 copy.13
  29.7 0.1 reshape.97
  29.8 0.1 copy.12
  29.9 0.0 copy-done.5
  29.9 0.1 copy.14
  29.9 0.1 eq.54
  30.0 0.1 fusion.23
  30.2 0.2 select_reduce_fusion
  30.4 0.1 iota_compare_fusion.2
  30.4 0.1 iota_compare_fusion.1
  30.5 64.4 %collective-permute-done.2 = bf16[3,1,8,256,256]{4,3,2,1,0:T(8,128)(2,1)} collective-permute-done((bf16[3,1,8,256,256]{4,3,2,1,0:T(8,128)(2,1)}, bf16[3,1,8,256,256]{4,3,2,1,0:T(8,128)(2,1)}, u32[]{:S(2)}, u32[]{:S(2)}) %collective-permute-start.2) | collective-permute-done | bytes 3145760 | tf_op jit(solution)/shard_map/ppermute | solution.py:14
  94.9 4.6 %collective-permute-done.3 = bf16[3,1,8,256,256]{4,3,2,1,0:T(8,128)(2,1)} collective-permute-done((bf16[3,1,8,256,256]{4,3,2,1,0:T(8,128)(2,1)}, bf16[3,1,8,256,256]{4,3,2,1,0:T(8,128)(2,1)}, u32[]{:S(2)}, u32[]{:S(2)}) %collective-permute-start.3) | collective-permute-done | bytes 3145760 | tf_op jit(solution)/shard_map/ppermute | solution.py:15
  99.6 7.7 %pad_maximum_fusion = bf16[3,3,8,256,256]{4,3,2,1,0:T(8,128)(2,1)} fusion(bf16[3,1,8,256,256]{4,3,2,1,0:T(8,128)(2,1)} %collective-permute-done.3, bf16[1,1,8,256,256]{4,3,2,1,0:T(8,128)(2,1)} %copy-done.2, bf16[1,1,8,256,256]{4,3,2,1,0:T(8,128)(2,1)} %bitcast.49, bf16[1,1,8,256,256]{4,3,2,1,0:T(8,128)(2,1)} %copy-done.1, ...), kind=kLoop, calls=%fused_computation.1 | loop fusion | flops 18874368 | bytes 18874368 | tf_op jit(solution)/shard_map/concatenate | solution.py:16
  107.3 6.2 %gather_fusion = bf16[24,256,256]{2,1,0:T(8,128)(2,1)} fusion(bf16[72,256,256]{2,1,0:T(8,128)(2,1)} %bitcast.44, s32[1024]{0:T(1024)S(1)} %pad_clamp_fusion), kind=kCustom, calls=%fused_computation | custom fusion | bytes 6291552 | tf_op jit(solution)/shard_map/jit(_take)/gather | solution.py:34
  113.5 5.7 %fusion.6 = bf16[8,3,256,256]{3,2,1,0:T(8,128)(2,1)} fusion(bf16[8,3,256,256]{3,2,1,0:T(8,128)(2,1)} %bitcast.51, pred[8,3]{1,0:T(8,128)(4,1)S(1)} %copy.12, bf16[8,3,256,256]{3,2,1,0:T(8,128)(2,1)S(1)} %copy-done, bf16[8,256,256]{2,1,0:T(8,128)(2,1)} %param.8), kind=kOutput, calls=%fused_computation.8 | convolution fusion | flops 1615331328 | bytes 10485784 | tf_op jit(solution)/shard_map/cjil,cjml->cjim/dot_general | solution.py:38
  119.2 3.8 %fusion.12 = bf16[8,3,64,256]{3,2,1,0:T(8,128)(2,1)} fusion(bf16[8,3,256,256]{3,2,1,0:T(8,128)(2,1)} %fusion.6, pred[8,64]{1,0:T(8,128)(4,1)S(1)} %iota_compare_fusion.2, bf16[8,256,64]{1,2,0:T(8,128)(2,1)S(1)} %copy-done.3, bf16[8,64,64]{2,1,0:T(8,128)(2,1)S(1)} %copy-done.4), kind=kOutput, calls=%fused_computation.12 | convolution fusion | flops 253624320 | bytes 5046784 | tf_op jit(solution)/shard_map/cab,cjbm->cjam/dot_general | solution.py:44
  123.0 2.7 %reshape.92 = bf16[24,64,2,128]{3,2,1,0:T(2,128)(2,1)} reshape(bf16[8,3,64,256]{3,2,1,0:T(8,128)(2,1)} %fusion.12) | data formatting | bytes 1572864 | tf_op jit(solution)/shard_map/reshape | solution.py:51
  125.7 2.0 convert_bitcast_fusion
  127.7 1.4 copy.16
  129.1 136.7 %all_to_all.5 = bf16[64,2,64,128]{3,2,1,0:T(8,128)(2,1)} all-to-all(bf16[64,2,64,128]{3,2,1,0:T(8,128)(2,1)S(1)} %bitcast.45), channel_id=1, replica_groups=mesh['sec'=8,'own'=32,'tile'=2] {'own','tile'}, dimensions={0} | all-to-all | bytes 4194304 | tf_op jit(solution)/shard_map/all_to_all | solution.py:64
  265.7 2.6 reduce_sum.22
  (15 shorter events, 0.1 us)
Async XLA Ops:
  0.0 113.5 %copy-start = (bf16[8,3,256,256]{3,2,1,0:T(8,128)(2,1)S(1)}, bf16[8,3,256,256]{3,2,1,0:T(8,128)(2,1)}, u32[]{:S(2)}) copy-start(bf16[8,3,256,256]{3,2,1,0:T(8,128)(2,1)} %param.7) | copy-start | bytes 9437188
  0.0 29.5 %copy-start.6 = (s32[8,3]{0,1:T(4,128)S(1)}, s32[8,3]{0,1:T(4,128)}, u32[]{:S(2)}) copy-start(s32[8,3]{0,1:T(4,128)} %param.11) | copy-start | bytes 292
  0.0 29.9 %copy-start.5 = (s32[8,3]{0,1:T(4,128)S(1)}, s32[8,3]{0,1:T(4,128)}, u32[]{:S(2)}) copy-start(s32[8,3]{0,1:T(4,128)} %param.13) | copy-start | bytes 292
  0.0 30.3 %copy-start.7 = (s32[8]{0:T(128)S(1)}, s32[8]{0:T(128)}, u32[]{:S(2)}) copy-start(s32[8]{0:T(128)} %param.12) | copy-start | bytes 100
  0.0 16.6 %collective-permute-start = (bf16[1,1,8,256,256]{4,3,2,1,0:T(8,128)(2,1)}, bf16[1,1,8,256,256]{4,3,2,1,0:T(8,128)(2,1)S(1)}, u32[]{:S(2)}, u32[]{:S(2)}) collective-permute-start(bf16[1,1,8,256,256]{4,3,2,1,0:T(8,128)(2,1)} %bitcast.46), channel_id=1, source_target_pairs={{0,64},{64,128},{128,192},{192,256},{256,320},{320,384},{384,448},... | collective-permute-start | bytes 3145736 | tf_op jit(solution)/shard_map/ppermute | solution.py:14
  2.2 16.3 %collective-permute-start.1 = (bf16[1,1,8,256,256]{4,3,2,1,0:T(8,128)(2,1)}, bf16[1,1,8,256,256]{4,3,2,1,0:T(8,128)(2,1)S(1)}, u32[]{:S(2)}, u32[]{:S(2)}) collective-permute-start(bf16[1,1,8,256,256]{4,3,2,1,0:T(8,128)(2,1)} %bitcast.47), channel_id=1, source_target_pairs={{64,0},{128,64},{192,128},{256,192},{320,256},{384,320},{448,384},... | collective-permute-start | bytes 3145736 | tf_op jit(solution)/shard_map/ppermute | solution.py:15
  16.6 5.5 %copy-start.1 = (bf16[1,1,8,256,256]{4,3,2,1,0:T(8,128)(2,1)}, bf16[1,1,8,256,256]{4,3,2,1,0:T(8,128)(2,1)S(1)}, u32[]{:S(2)}) copy-start(bf16[1,1,8,256,256]{4,3,2,1,0:T(8,128)(2,1)S(1)} %collective-permute-done) | copy-start | bytes 3145732
  18.5 3.6 %copy-start.2 = (bf16[1,1,8,256,256]{4,3,2,1,0:T(8,128)(2,1)}, bf16[1,1,8,256,256]{4,3,2,1,0:T(8,128)(2,1)S(1)}, u32[]{:S(2)}) copy-start(bf16[1,1,8,256,256]{4,3,2,1,0:T(8,128)(2,1)S(1)} %collective-permute-done.1) | copy-start | bytes 3145732
  22.1 72.9 %collective-permute-start.2 = (bf16[3,1,8,256,256]{4,3,2,1,0:T(8,128)(2,1)}, bf16[3,1,8,256,256]{4,3,2,1,0:T(8,128)(2,1)}, u32[]{:S(2)}, u32[]{:S(2)}) collective-permute-start(bf16[3,1,8,256,256]{4,3,2,1,0:T(8,128)(2,1)} %pad_maximum_fusion.1), channel_id=1, source_target_pairs={{0,2},{2,4},{4,6},{6,8},{8,10},{10,12},{12,14},{14,16},{16,18},{18... | collective-permute-start | bytes 9437192 | tf_op jit(solution)/shard_map/ppermute | solution.py:14
  26.3 73.2 %collective-permute-start.3 = (bf16[3,1,8,256,256]{4,3,2,1,0:T(8,128)(2,1)}, bf16[3,1,8,256,256]{4,3,2,1,0:T(8,128)(2,1)}, u32[]{:S(2)}, u32[]{:S(2)}) collective-permute-start(bf16[3,1,8,256,256]{4,3,2,1,0:T(8,128)(2,1)} %pad_maximum_fusion.1), channel_id=1, source_target_pairs={{2,0},{4,2},{6,4},{8,6},{10,8},{12,10},{14,12},{16,14},{18,16},{20... | collective-permute-start | bytes 9437192 | tf_op jit(solution)/shard_map/ppermute | solution.py:15
  113.5 5.7 %copy-start.3 = (bf16[8,256,64]{1,2,0:T(8,128)(2,1)S(1)}, bf16[8,256,64]{1,2,0:T(8,128)(2,1)}, u32[]{:S(2)}) copy-start(bf16[8,256,64]{1,2,0:T(8,128)(2,1)} %param.10) | copy-start | bytes 786436
  113.5 5.7 %copy-start.4 = (bf16[8,64,64]{2,1,0:T(8,128)(2,1)S(1)}, bf16[8,64,64]{2,1,0:T(8,128)(2,1)}, u32[]{:S(2)}) copy-start(bf16[8,64,64]{2,1,0:T(8,128)(2,1)} %param.9) | copy-start | bytes 196612
where the time goes:
time: 269 us; the launch traced here: 268 us
  blocking collectives  137 us (51%)
  waiting for transfers between devices  81.7 us (30%)
  other arithmetic  14.4 us (5%)
  starting transfers between devices  13.3 us (5%)
  matrix products  11.5 us (4%)
  local copies, waits for them, and re-layouts  10.7 us (4%)
    all_to_all x1, blocking collectives, on_device(): lax.all_to_all(send_slots, ('own', 'tile'), split_axis=0, concat_axis=0,...  137 us
    ppermute x2, waiting for transfers between devices, padded(): before = lax.ppermute(last, axis, up)  75.2 us
    concatenate x2, other arithmetic, padded(): array = jnp.concatenate([before, array, after], axis=dim)  11.3 us
    ppermute x2, starting transfers between devices, padded(): after = lax.ppermute(initial, axis, down)  6.83 us
    ppermute x2, waiting for transfers between devices, padded(): after = lax.ppermute(initial, axis, down)  6.51 us
    ppermute x2, starting transfers between devices, padded(): before = lax.ppermute(last, axis, up)  6.46 us
    gather x1, local copies, waits for them, and re-layouts, on_device(): near_factors = jnp.take(window, local_index, axis=0)  6.16 us
    dot_general x1, matrix products, on_device(): jnp.einsum('cjil,cjml->cjim', left, near_factors, preferred_element_type=...  5.72 us
  transfers between devices with their start and end apart: 4, of which 4 were waited for; matrix products, arithmetic and copies ran while one was open for 0% of the time, Pallas kernels for 0%

commit v1 on v0

v1 whole, which is shorter than its diff:
```python
import jax
import jax.numpy as jnp
from jax import lax
from jax.experimental import pallas as pl
from jax.experimental.pallas import tpu as pltpu
from jax.sharding import PartitionSpec as P

MESH = pl.DeviceIdType.MESH
F32 = jnp.float32
BF16 = jnp.bfloat16
CL, NB, CW, K = 8, 3, 256, 64
HALF = CW // 2
RING = 8
OWNERS = 32
SECTIONS = 8
PER_SECTION = 512
EMPTY = 32


def dot(a, b):
    return lax.dot_general(a, b, (((1,), (0,)), ((), ())), preferred_element_type=F32)


def dot_t(a, b):
    return lax.dot_general(a, b, (((1,), (1,)), ((), ())), preferred_element_type=F32)


def kernel(couple, factors, reflect, wy, nid, rank, mmap, out,
           couple_v, fac, refl_v, wy_v, sec_top, sec_bot, zs, zr, tab_s, tab_v, tab, coarse, total,
           za3, za4, zad, zas, zat, ya3, ya4, yad, yas, yat, pa, pb, ra, rb,
           load_sem, ss, rs):
    sec, own, tile = lax.axis_index("sec"), lax.axis_index("own"), lax.axis_index("tile")
    z, y = lax.rem(own, RING), (own // RING) * 2 + tile

    def zdev(d):
        return {"own": (own // RING) * RING + lax.rem(z + d + RING, RING)}

    def ydev(d):
        to = lax.rem(y + d + RING, RING)
        return {"own": (to // 2) * RING + z, "tile": lax.rem(to, 2)}

    def sdev(d):
        return {"sec": lax.rem(sec + d + SECTIONS, SECTIONS)}

    has_low, has_up = own > 0, own < OWNERS - 1
    low = jnp.where(has_low, own - 1, own + 1)
    up = jnp.where(has_up, own + 1, own - 1)

    loads = [pltpu.make_async_copy(factors, fac, load_sem.at[0]),
             pltpu.make_async_copy(wy, wy_v, load_sem.at[1]),
             pltpu.make_async_copy(reflect, refl_v, load_sem.at[2])]
    for part in range(2):
        at = pl.ds(part * 4, 4)
        loads.append(pltpu.make_async_copy(couple.at[at], couple_v.at[at], load_sem.at[3 + part]))
    for copy in loads:
        copy.start()

    barrier = pltpu.get_barrier_semaphore()

    def greet(to):
        pl.semaphore_signal(barrier, inc=1, device_id=to, device_id_type=MESH)

    greet(sdev(1))
    greet(sdev(-1))

    @pl.when(has_low)
    def _():
        greet({"own": own - 1})

    @pl.when(has_up)
    def _():
        greet({"own": own + 1})

    for d in (1, -1, 2, -2, 3, -3, 4):
        greet(zdev(d))
        greet(ydev(d))

    lane = lax.broadcasted_iota(jnp.int32, (8, 128), 1)
    row = lax.broadcasted_iota(jnp.int32, (8, 128), 0)

    def table(groups):
        first = jnp.full((8, 128), EMPTY, jnp.int32)
        second = jnp.full((8, 128), EMPTY, jnp.int32)
        local = jnp.zeros((8, 128), jnp.int32)
        for j, base, wanted in groups:
            for c in range(CL):
                hit = lane == mmap[j, c]
                if wanted is not None:
                    hit = hit & wanted
                second = jnp.where(hit & (first != EMPTY), base + c, second)
                first = jnp.where(hit & (first == EMPTY), base + c, first)
                local = jnp.where(lane == base + c, nid[j, c] & (CL - 1), local)
        return jnp.where(row == 0, first, jnp.where(row == 1, second, local))

    at_low_end = jnp.full((8, 128), own, jnp.int32) == 0
    at_up_end = jnp.full((8, 128), own, jnp.int32) == OWNERS - 1
    tab_s[0] = table([(0, 8, None), (1, 24, at_up_end)])
    tab_s[1] = table([(1, 16, None), (0, 24, at_low_end)])
    tab_v[2] = table([(2, 0, None)])
    nothing = jnp.where(row < 2, EMPTY, 0)

    @pl.when(jnp.logical_not(has_low))
    def _():
        tab_v[0] = nothing

    @pl.when(jnp.logical_not(has_up))
    def _():
        tab_v[1] = nothing

    coarse[EMPTY] = jnp.zeros((K, CW), F32)
    edges = has_low.astype(jnp.int32) + has_up.astype(jnp.int32)
    pl.semaphore_wait(barrier, 2 + 14 + edges)

    count = [0]

    def remote(src, dst, to):
        i = count[0]
        count[0] += 1
        return pltpu.make_async_remote_copy(src_ref=src, dst_ref=dst, send_sem=ss.at[i], recv_sem=rs.at[i],
                                            device_id=to, device_id_type=MESH)

    sends = []
    for side, d in ((0, 1), (1, -1)):
        at = pl.ds(side * CL, CL)
        sends.append(remote(factors.at[:, pl.ds(HALF, HALF), :], sec_bot.at[at], sdev(d)))
        sends.append(remote(factors.at[:, pl.ds(0, HALF), pl.ds(0, HALF)], sec_top.at[at], sdev(d)))
    for copy in sends:
        copy.start()
    sec_copies = list(sends)
    to_low = remote(tab_s.at[0], tab_v.at[1], {"own": low})
    to_up = remote(tab_s.at[1], tab_v.at[0], {"own": up})

    @pl.when(has_low)
    def _():
        to_low.start()

    @pl.when(has_up)
    def _():
        to_up.start()

    base_sem = count[0]
    count[0] += 6
    for copy in loads[:3]:
        copy.wait()
    r_iota = lax.broadcasted_iota(jnp.int32, (K, CW), 0)
    c_iota = lax.broadcasted_iota(jnp.int32, (K, CW), 1)
    eye = jnp.where(r_iota == c_iota, 1.0, 0.0)
    z_copies = []
    low_group = jnp.where(has_low, 0, 2)
    up_group = jnp.where(has_up, 1, 2)
    for part in range(2):
        loads[3 + part].wait()
        tops = []
        for c in range(part * 4, part * 4 + 4):
            t = eye - dot(refl_v[c], wy_v[c])
            t = jnp.where(r_iota < rank[c], t, 0.0).astype(BF16)
            tops.append(dot(t, fac[c]).astype(BF16))
        for j in range(NB):
            for c in range(part * 4, part * 4 + 4):
                zs[j, c] = dot(tops[c - part * 4], couple_v[c, j]).astype(BF16)
            if j < 2:
                group = (low_group, up_group)[j]
                at = pl.ds(part * 4, 4)
                copy = pltpu.make_async_remote_copy(
                    src_ref=zs.at[j, at], dst_ref=zr.at[group, at], send_sem=ss.at[base_sem + 2 * j + part],
                    recv_sem=rs.at[base_sem + 2 * group + part], device_id={"own": (low, up)[j]}, device_id_type=MESH)
                copy.start()
                z_copies.append(copy)

    @pl.when(has_low)
    def _():
        to_low.wait_send()
        to_up_like = to_up
        to_up_like.wait_recv()

    @pl.when(has_up)
    def _():
        to_up.wait_send()
        to_low.wait_recv()

    tab_copy = pltpu.make_async_copy(tab_v, tab, load_sem.at[5])
    tab_copy.start()
    tab_copy.wait()

    for copy in sec_copies:
        copy.wait()
    for c in range(CL):
        n = nid[2, c]
        at = (n & (CL - 1)) + jnp.where(n // PER_SECTION > sec, CL, 0)
        coarse[c, :, pl.ds(0, HALF)] = dot_t(zs[2, c, :, pl.ds(0, HALF)], sec_top[at])
        coarse[c, :, pl.ds(HALF, HALF)] = dot_t(zs[2, c], sec_bot[at])

    def landed(group, part):
        at = pl.ds(part * 4, 4)
        pltpu.make_async_remote_copy(
            src_ref=zs.at[0, at], dst_ref=zr.at[group, at], send_sem=ss.at[base_sem], recv_sem=rs.at[base_sem + 2 * group + part],
            device_id={"own": low}, device_id_type=MESH).wait_recv()

    def finish(group, base, side, part):
        for c in range(part * 4, part * 4 + 4):
            at = tab[side, 2, base + c]
            coarse[base + c] = dot_t(zr[group, c], fac[at])

    for part in range(2):
        @pl.when(has_up)
        def _():
            landed(0, part)
            finish(0, 8, 1, part)

        @pl.when(has_low)
        def _():
            landed(1, part)
            finish(1, 16, 0, part)

    @pl.when(own == 1)
    def _():
        for part in range(2):
            landed(2, part)
            finish(2, 24, 0, part)

    @pl.when(own == OWNERS - 2)
    def _():
        for part in range(2):
            landed(2, part)
            finish(2, 24, 1, part)

    for yh in range(4):
        def gather(zz, _):
            m = yh * RING + zz
            acc = coarse[tab[0, 0, m]] + coarse[tab[0, 1, m]]
            acc = acc + coarse[tab[1, 0, m]] + coarse[tab[1, 1, m]]
            acc = acc + coarse[tab[2, 0, m]] + coarse[tab[2, 1, m]]
            total[yh, zz] = acc.astype(BF16)
            return 0

        lax.fori_loop(0, RING, gather, 0)

    def zpiece(d, part=None):
        rows = pl.ds(0, 4) if part is None else pl.ds(2 * part, 2)
        return total.at[rows, lax.rem(z + d + RING, RING), pl.ds(0, 32), :]

    def ypiece(d, part=None):
        to = lax.rem(y + d + RING, RING)
        rows = pl.ds(0, 8) if part is None else pl.ds(4 * part, 4)
        return total.at[to // 2, rows, pl.ds(32, 32), pl.ds(pl.multiple_of(lax.rem(to, 2) * HALF, HALF), HALF)]

    axes = ((zpiece, zdev, za3, za4, zad, zas, zat, 2), (ypiece, ydev, ya3, ya4, yad, yas, yat, 4))
    fours, threes, ones = [], [], []
    for piece, dev, b3, b4, bd, _, _, _ in axes:
        for side, s in ((0, 1), (1, -1)):
            fours.append(remote(piece(4 * s, side), b4.at[side], dev(2 * s)))
            threes.append(remote(piece(3 * s), b3.at[side], dev(s)))
            ones.append(remote(piece(s), bd.at[side], dev(s)))
    for copy in fours + threes + ones:
        copy.start()
    twos = []
    for a, (piece, dev, b3, b4, bd, bs, bt, half) in enumerate(axes):
        for side, s in ((0, 1), (1, -1)):
            i = 2 * a + side
            fours[i].wait_recv()
            threes[i].wait_recv()
            near = pl.ds(half * side, half)
            far = pl.ds(half * (1 - side), half)
            mine = piece(2 * s)
            b3s = b3.at[side]
            bts = bt.at[side]
            bts[near] = (mine[near].astype(F32) + b3s[near].astype(F32) + b4[side].astype(F32)).astype(BF16)
            bts[far] = (mine[far].astype(F32) + b3s[far].astype(F32)).astype(BF16)
            copy = remote(bts, bs.at[side], dev(2 * s))
            copy.start()
            twos.append(copy)
    for copy in ones + twos:
        copy.wait_recv()
    sum_a = zpiece(0)[...].astype(F32)
    sum_b = ypiece(0)[...].astype(F32)
    for side in range(2):
        sum_a = sum_a + zad[side].astype(F32) + zas[side].astype(F32)
        sum_b = sum_b + yad[side].astype(F32) + yas[side].astype(F32)
    for part in range(2):
        for yh in range(4):
            pa[2 * yh + part] = sum_a[yh, :, part * HALF:(part + 1) * HALF].astype(BF16)
    pb[...] = sum_b.astype(BF16)

    last = []
    for d in (4, 3, 5, 2, 6, 1, 7):
        last.append(remote(pa.at[lax.rem(y + d, RING)], ra.at[d - 1], ydev(d)))
        last.append(remote(pb.at[lax.rem(z + d, RING)], rb.at[d - 1], zdev(d)))
    for copy in last:
        copy.start()
    for copy in last:
        copy.wait_recv()
    done_a, done_b = pa[y].astype(F32), pb[z].astype(F32)
    for d in range(RING - 1):
        done_a = done_a + ra[d].astype(F32)
        done_b = done_b + rb[d].astype(F32)
    out[0, 0, pl.ds(0, 32), :] = done_a.astype(BF16)
    out[0, 0, pl.ds(32, 32), :] = done_b.astype(BF16)
    for copy in z_copies + fours + threes + ones + twos + last:
        copy.wait_send()


def on_device(couple, factors, top_reflect, wy_factor, neighbour_ids, kept_rank, merge_map):
    hbm, smem, vmem = (pl.BlockSpec(memory_space=s) for s in (pl.ANY, pltpu.SMEM, pltpu.VMEM))
    v = lambda *shape: pltpu.VMEM(shape, BF16)
    return pl.pallas_call(
        kernel,
        name="merge_level",
        out_shape=jax.ShapeDtypeStruct((1, 1, K, HALF), BF16),
        in_specs=[hbm, hbm, hbm, hbm, smem, smem, smem],
        out_specs=vmem,
        scratch_shapes=[
            v(CL, NB, CW, CW), v(CL, CW, CW), v(CL, K, K), v(CL, K, CW),
            v(2 * CL, HALF, HALF), v(2 * CL, HALF, CW),
            v(NB, CL, K, CW), v(3, CL, K, CW),
            pltpu.VMEM((2, 8, 128), jnp.int32), pltpu.VMEM((3, 8, 128), jnp.int32), pltpu.SMEM((3, 8, 128), jnp.int32),
            pltpu.VMEM((EMPTY + 1, K, CW), F32), v(4, RING, K, CW),
            v(2, 4, 32, CW), v(2, 2, 32, CW), v(2, 4, 32, CW), v(2, 4, 32, CW), v(2, 4, 32, CW),
            v(2, 8, 32, HALF), v(2, 4, 32, HALF), v(2, 8, 32, HALF), v(2, 8, 32, HALF), v(2, 8, 32, HALF),
            v(8, 32, HALF), v(8, 32, HALF), v(7, 32, HALF), v(7, 32, HALF),
            pltpu.SemaphoreType.DMA((6,)), pltpu.SemaphoreType.DMA((42,)), pltpu.SemaphoreType.DMA((42,)),
        ],
        compiler_params=pltpu.CompilerParams(collective_id=0, has_side_effects=True, vmem_limit_bytes=62 << 20),
    )(couple, factors, top_reflect, wy_factor.transpose(0, 2, 1), neighbour_ids.T, kept_rank, merge_map.T)


def solution(mesh):
    own = ("sec", "own", "tile")
    in_specs = (P(own, None, None, None), P(own, None, None), P(own, None, None), P(own, None, None),
                P(own, None), P(own), P(own, None))
    return jax.shard_map(on_device, mesh=mesh, in_specs=in_specs, out_specs=P("sec", "own", None, "tile"), check_vma=False)
```

time: 269 us -> 49.7 us (0.18)
  the two profiles are of different devices: /device:TPU:68 before, /device:TPU:6 now
where the time goes in v1:
time: 49.7 us; the launch traced here: 49.5 us
  Pallas kernels  48.1 us (97%)
  local copies, waits for them, and re-layouts  1.32 us (3%)
    pallas_call x1, Pallas kernels, on_device(): pl.pallas_call(kernel, name='merge_level', out_shape=jax.ShapeDtypeStruct...  48.1 us
    unnamed x1, local copies, waits for them, and re-layouts  1.32 us

profile of v1, /device:TPU:6, one launch (start us, length us, event | category | flops | bytes accessed | tf_op | source)
XLA Modules:
  0.0 49.5 jit_solution(17286314558489257627)
XLA Ops:
  0.0 48.1 %merge_level.1 = bf16[1,1,64,128]{3,2,1,0:T(8,128)(2,1)} custom-call(bf16[8,3,256,256]{3,2,1,0:T(8,128)(2,1)} %couple.1, bf16[8,256,256]{2,1,0:T(8,128)(2,1)} %factors.1, bf16[8,64,64]{2,1,0:T(8,128)(2,1)} %reflect.1, bf16[8,64,256]{2,1,0:T(8,128)(2,1)} %bitcast.3, s32[3,8]{1,0:T(4,128)} %bitcast.4, s32[8]{0:T(128)} %rank.1, s32[3,8]{1,0:T(4,128)} %bitcast.5), custom_call_target="tpu_custom_call" | custom-call | tf_op jit(solution)/shard_map/merge_level/pallas_call | solution.py:305
  48.1 1.3 %copy.9 = bf16[1,1,64,128]{3,2,1,0:T(8,128)(2,1)} copy(bf16[1,1,64,128]{3,2,1,0:T(8,128)(2,1)} %merge_level.1) | data formatting | bytes 32768

commit v2 on v1

v2 whole, which is shorter than its diff:
```python
import jax
import jax.numpy as jnp
from jax import lax
from jax.experimental import pallas as pl
from jax.experimental.pallas import tpu as pltpu
from jax.sharding import PartitionSpec as P

MESH = pl.DeviceIdType.MESH
F32 = jnp.float32
BF16 = jnp.bfloat16
CL, NB, CW, K = 8, 3, 256, 64
HALF = CW // 2
RING = 8
OWNERS = 32
SECTIONS = 8
PER_SECTION = 512
PARTS = 4
PER = CL // PARTS
SEMS = 72
EMPTY = 32


def dot(a, b):
    return lax.dot_general(a, b, (((1,), (0,)), ((), ())), preferred_element_type=F32)


def dot_t(a, b):
    return lax.dot_general(a, b, (((1,), (1,)), ((), ())), preferred_element_type=F32)


def kernel(couple, factors, reflect, wy, nid_h, rank_h, mmap_h, out,
           nid, rank, mmap, couple_v, fac, refl_v, wy_v, pack, diag, sec_b, sec_u, sec_d, zs, zr, fw, tab_s, tab_v, tab, coarse, total,
           za3, za4, zad, zas, zat, ya3, ya4, yad, yas, yat, pa, pb, ra, rb,
           load_sem, ss, rs):
    sec, own, tile = lax.axis_index("sec"), lax.axis_index("own"), lax.axis_index("tile")
    z, y = lax.rem(own, RING), (own // RING) * 2 + tile

    def zdev(d):
        return {"own": (own // RING) * RING + lax.rem(z + d + RING, RING)}

    def ydev(d):
        to = lax.rem(y + d + RING, RING)
        return {"own": (to // 2) * RING + z, "tile": lax.rem(to, 2)}

    def sdev(d):
        return {"sec": lax.rem(sec + d + SECTIONS, SECTIONS)}

    has_low, has_up = own > 0, own < OWNERS - 1
    low = jnp.where(has_low, own - 1, own + 1)
    up = jnp.where(has_up, own + 1, own - 1)

    ints = [pltpu.make_async_copy(a, b, load_sem.at[6 + i]) for i, (a, b) in enumerate(((mmap_h, mmap), (nid_h, nid), (rank_h, rank)))]
    loads = [pltpu.make_async_copy(factors, fac, load_sem.at[0]),
             pltpu.make_async_copy(wy, wy_v, load_sem.at[1]),
             pltpu.make_async_copy(reflect, refl_v, load_sem.at[2])]
    couples = []
    for part in range(PARTS):
        at = pl.ds(part * PER, PER)
        couples.append(pltpu.make_async_copy(couple.at[at], couple_v.at[at], load_sem.at[9 + part]))
    for copy in ints + loads + couples:
        copy.start()

    barrier = pltpu.get_barrier_semaphore()

    def greet(to):
        pl.semaphore_signal(barrier, inc=1, device_id=to, device_id_type=MESH)

    greet(sdev(1))
    greet(sdev(-1))

    @pl.when(has_low)
    def _():
        greet({"own": own - 1})

    @pl.when(has_up)
    def _():
        greet({"own": own + 1})

    for d in (1, -1, 2, -2, 3, -3, 4):
        greet(zdev(d))
        greet(ydev(d))

    for copy in ints:
        copy.wait()
    lane = lax.broadcasted_iota(jnp.int32, (8, 128), 1)
    row = lax.broadcasted_iota(jnp.int32, (8, 128), 0)

    def table(groups):
        first = jnp.full((8, 128), EMPTY, jnp.int32)
        second = jnp.full((8, 128), EMPTY, jnp.int32)
        local = jnp.zeros((8, 128), jnp.int32)
        for j, base, wanted in groups:
            for c in range(CL):
                hit = lane == mmap[j, c]
                if wanted is not None:
                    hit = hit & wanted
                second = jnp.where(hit & (first != EMPTY), base + c, second)
                first = jnp.where(hit & (first == EMPTY), base + c, first)
                local = jnp.where(lane == base + c, nid[j, c] & (CL - 1), local)
        return jnp.where(row == 0, first, jnp.where(row == 1, second, local))

    at_low_end = jnp.full((8, 128), own, jnp.int32) == 0
    at_up_end = jnp.full((8, 128), own, jnp.int32) == OWNERS - 1
    tab_s[0] = table([(0, 8, None), (1, 24, at_up_end)])
    tab_s[1] = table([(1, 16, None), (0, 24, at_low_end)])
    tab_v[2] = table([(2, 0, None)])
    nothing = jnp.where(row < 2, EMPTY, 0)

    @pl.when(jnp.logical_not(has_low))
    def _():
        tab_v[0] = nothing

    @pl.when(jnp.logical_not(has_up))
    def _():
        tab_v[1] = nothing

    coarse[EMPTY] = jnp.zeros((K, CW), F32)
    edges = has_low.astype(jnp.int32) + has_up.astype(jnp.int32)
    pl.semaphore_wait(barrier, 2 + 14 + edges)

    count = [0]

    def remote(src, dst, to):
        i = count[0]
        count[0] += 1
        return pltpu.make_async_remote_copy(src_ref=src, dst_ref=dst, send_sem=ss.at[i], recv_sem=rs.at[i],
                                            device_id=to, device_id_type=MESH)

    loads[0].wait()
    sec_copies = []
    for side, d in ((0, 1), (1, -1)):
        copy = remote(fac.at[:, pl.ds(HALF, HALF), pl.ds(0, HALF)], sec_b.at[pl.ds(side * CL, CL)], sdev(d))
        copy.start()
        sec_copies.append(copy)
    sq_r = lax.broadcasted_iota(jnp.int32, (HALF, HALF), 0)
    sq_c = lax.broadcasted_iota(jnp.int32, (HALF, HALF), 1)
    for c in range(CL):
        lower = fac[c, pl.ds(HALF, HALF), pl.ds(HALF, HALF)].astype(F32)
        diag[pl.ds(c, 1), :] = jnp.sum(jnp.where(sq_r == sq_c, lower, 0.0), axis=0, keepdims=True)
        upper = fac[c, pl.ds(0, HALF), pl.ds(0, HALF)].astype(F32)
        pack[c] = jnp.where(sq_r >= sq_c, upper, lower.T).astype(BF16)
    for side, d in ((0, 1), (1, -1)):
        at = pl.ds(side * CL, CL)
        for copy in (remote(pack, sec_u.at[at], sdev(d)), remote(diag, sec_d.at[at], sdev(d))):
            copy.start()
            sec_copies.append(copy)
    to_low = remote(tab_s.at[0], tab_v.at[1], {"own": low})
    to_up = remote(tab_s.at[1], tab_v.at[0], {"own": up})

    @pl.when(has_low)
    def _():
        to_low.start()

    @pl.when(has_up)
    def _():
        to_up.start()

    base_sem = count[0]
    count[0] += 3 * PARTS
    fw_sem = count[0]
    count[0] += 2
    on_sem = count[0]
    count[0] += 2
    for copy in loads[1:]:
        copy.wait()
    r_iota = lax.broadcasted_iota(jnp.int32, (K, CW), 0)
    c_iota = lax.broadcasted_iota(jnp.int32, (K, CW), 1)
    eye = jnp.where(r_iota == c_iota, 1.0, 0.0)
    low_group = jnp.where(has_low, 0, 2)
    up_group = jnp.where(has_up, 1, 2)
    cross_low = (z == 0) & has_low
    cross_up = (z == RING - 1) & has_up
    tops = []
    for c in range(CL):
        t = eye - dot(refl_v[c], wy_v[c])
        t = jnp.where(r_iota < rank[c], t, 0.0).astype(BF16)
        tops.append(dot(t, fac[c]).astype(BF16))
    z_sends = []

    def z_send(j, part):
        at = pl.ds(part * PER, PER)
        group = (low_group, up_group)[j]
        to = (low, up)[j]
        crossing = (cross_low, cross_up)[j]
        plain = pltpu.make_async_remote_copy(
            src_ref=zs.at[j, at], dst_ref=zr.at[group, at], send_sem=ss.at[base_sem + j * PARTS + part],
            recv_sem=rs.at[base_sem + group * PARTS + part], device_id={"own": to}, device_id_type=MESH)
        z_sends.append(plain)
        if part >= 2:
            plain.start()
            return
        by_way = pltpu.make_async_remote_copy(
            src_ref=zs.at[j, at], dst_ref=fw.at[pl.ds(part * PER, PER)], send_sem=ss.at[base_sem + j * PARTS + part],
            recv_sem=rs.at[fw_sem + part], device_id=zdev((-1, 1)[j]), device_id_type=MESH)

        @pl.when(crossing)
        def _():
            by_way.start()

        @pl.when(jnp.logical_not(crossing))
        def _():
            plain.start()

    for part in range(PARTS):
        couples[part].wait()
        for j in (1, 0, 2):
            for c in range(part * PER, part * PER + PER):
                zs[j, c] = dot(tops[c], couple_v[c, j]).astype(BF16)
            if j < 2:
                z_send(j, part)

    def send_on(group, to, part):
        at = pl.ds(part * PER, PER)
        return pltpu.make_async_remote_copy(
            src_ref=fw.at[at], dst_ref=zr.at[group, at], send_sem=ss.at[on_sem + part],
            recv_sem=rs.at[base_sem + group * PARTS + part], device_id={"own": to}, device_id_type=MESH)

    def fw_landed(part):
        at = pl.ds(part * PER, PER)
        pltpu.make_async_remote_copy(src_ref=zs.at[0, at], dst_ref=fw.at[at], send_sem=ss.at[base_sem], recv_sem=rs.at[fw_sem + part],
                                     device_id=zdev(1), device_id_type=MESH).wait_recv()

    def landed(group, part):
        at = pl.ds(part * PER, PER)
        pltpu.make_async_remote_copy(
            src_ref=zs.at[0, at], dst_ref=zr.at[group, at], send_sem=ss.at[base_sem], recv_sem=rs.at[base_sem + group * PARTS + part],
            device_id={"own": low}, device_id_type=MESH).wait_recv()

    on_up = (z == 0) & (own < OWNERS - RING)
    on_low = (z == RING - 1) & (own >= RING)
    for part in range(2):
        @pl.when(on_up)
        def _():
            fw_landed(part)
            send_on(1, own + RING, part).start()

        @pl.when(on_low)
        def _():
            fw_landed(part)
            send_on(0, own - RING, part).start()

    @pl.when(has_low)
    def _():
        to_low.wait_send()
        to_up_like = to_up
        to_up_like.wait_recv()

    @pl.when(has_up)
    def _():
        to_up.wait_send()
        to_low.wait_recv()

    tab_copy = pltpu.make_async_copy(tab_v, tab, load_sem.at[5])
    tab_copy.start()
    tab_copy.wait()

    for copy in sec_copies:
        copy.wait()
    for c in range(CL):
        n = nid[2, c]
        at = (n & (CL - 1)) + jnp.where(n // PER_SECTION > sec, CL, 0)
        square = sec_u[at].astype(F32)
        line = sec_d[pl.ds(at, 1), :]
        head = jnp.where(sq_r >= sq_c, square, 0.0).astype(BF16)
        tail = jnp.where(sq_r < sq_c, square, jnp.where(sq_r == sq_c, line, 0.0)).astype(BF16)
        near, far = zs[2, c, :, pl.ds(0, HALF)], zs[2, c, :, pl.ds(HALF, HALF)]
        coarse[c, :, pl.ds(0, HALF)] = dot_t(near, head)
        coarse[c, :, pl.ds(HALF, HALF)] = dot_t(near, sec_b[at]) + dot(far, tail)

    def finish(group, base, side, part):
        for c in range(part * PER, part * PER + PER):
            at = tab[side, 2, base + c]
            coarse[base + c] = dot_t(zr[group, c], fac[at])

    def take(group, base, side):
        for part in range(PARTS):
            landed(group, part)
        for part in range(PARTS):
            finish(group, base, side, part)

    @pl.when(has_up)
    def _():
        take(0, 8, 1)

    @pl.when(has_low)
    def _():
        take(1, 16, 0)

    @pl.when(own == 1)
    def _():
        take(2, 24, 0)

    @pl.when(own == OWNERS - 2)
    def _():
        take(2, 24, 1)

    for yh in range(4):
        def gather(zz, _):
            m = yh * RING + zz
            acc = coarse[tab[0, 0, m]] + coarse[tab[0, 1, m]]
            acc = acc + coarse[tab[1, 0, m]] + coarse[tab[1, 1, m]]
            acc = acc + coarse[tab[2, 0, m]] + coarse[tab[2, 1, m]]
            total[yh, zz] = acc.astype(BF16)
            return 0

        lax.fori_loop(0, RING, gather, 0)

    def zpiece(d, half=None, part=None):
        rows = pl.ds(0, 32) if half is None else pl.ds(16 * half, 16)
        which = pl.ds(0, 4) if part is None else pl.ds(2 * part, 2)
        return total.at[which, lax.rem(z + d + RING, RING), rows, :]

    def ypiece(d, half=None, part=None):
        to = lax.rem(y + d + RING, RING)
        rows = pl.ds(32, 32) if half is None else pl.ds(32 + 16 * half, 16)
        which = pl.ds(0, 8) if part is None else pl.ds(4 * part, 4)
        return total.at[to // 2, which, rows, pl.ds(pl.multiple_of(lax.rem(to, 2) * HALF, HALF), HALF)]

    axes = ((zpiece, zdev, za3, za4, zad, zas, zat, 2), (ypiece, ydev, ya3, ya4, yad, yas, yat, 4))
    ways = [(a, side, s) for a in range(2) for side, s in ((0, 1), (1, -1))]
    fours, threes, ones, twos = {}, {}, {}, {}
    for half in range(2):
        for a, side, s in ways:
            piece, dev, b3, b4 = axes[a][:4]
            fours[half, a, side] = remote(piece(4 * s, half, side), b4.at[half, side], dev(2 * s))
            fours[half, a, side].start()
        for a, side, s in ways:
            piece, dev, b3, b4 = axes[a][:4]
            threes[half, a, side] = remote(piece(3 * s, half), b3.at[half, side], dev(s))
            threes[half, a, side].start()
    for a, side, s in ways:
        threes[1, a, side].wait_send()
        ones[a, side] = remote(axes[a][0](s), axes[a][4].at[side], axes[a][1](s))
        ones[a, side].start()
    for half in range(2):
        for a, side, s in ways:
            piece, dev, b3, b4, _, bs, bt, n = axes[a]
            fours[half, a, side].wait_recv()
            threes[half, a, side].wait_recv()
            near, far = pl.ds(n * side, n), pl.ds(n * (1 - side), n)
            mine, third, to = piece(2 * s, half), b3.at[half, side], bt.at[half, side]
            to[near] = (mine[near].astype(F32) + third[near].astype(F32) + b4[half, side].astype(F32)).astype(BF16)
            to[far] = (mine[far].astype(F32) + third[far].astype(F32)).astype(BF16)
            twos[half, a, side] = remote(to, bs.at[half, side], dev(2 * s))
            twos[half, a, side].start()
    for copy in list(ones.values()) + list(twos.values()):
        copy.wait_recv()
    sums = []
    for piece, _, _, _, bd, bs, _, _ in axes:
        halves = []
        for half in range(2):
            rows = pl.ds(16 * half, 16)
            acc = piece(0, half)[...].astype(F32)
            for side in range(2):
                acc = acc + bd[side, :, rows, :].astype(F32) + bs[half, side].astype(F32)
            halves.append(acc)
        sums.append(jnp.concatenate(halves, axis=1))
    sum_a, sum_b = sums
    for part in range(2):
        for yh in range(4):
            pa[2 * yh + part] = sum_a[yh, :, part * HALF:(part + 1) * HALF].astype(BF16)
    pb[...] = sum_b.astype(BF16)

    last = []
    for d in (4, 3, 5, 2, 6, 1, 7):
        last.append(remote(pa.at[lax.rem(y + d, RING)], ra.at[d - 1], ydev(d)))
        last.append(remote(pb.at[lax.rem(z + d, RING)], rb.at[d - 1], zdev(d)))
    for copy in last:
        copy.start()
    for copy in last:
        copy.wait_recv()
    done_a, done_b = pa[y].astype(F32), pb[z].astype(F32)
    for d in range(RING - 1):
        done_a = done_a + ra[d].astype(F32)
        done_b = done_b + rb[d].astype(F32)
    out[0, 0, pl.ds(0, 32), :] = done_a.astype(BF16)
    out[0, 0, pl.ds(32, 32), :] = done_b.astype(BF16)
    late = [threes[0, a, side] for a, side, _ in ways]
    for copy in z_sends + list(fours.values()) + late + list(ones.values()) + list(twos.values()) + last:
        copy.wait_send()

    @pl.when(on_up | on_low)
    def _():
        for part in range(2):
            send_on(1, low, part).wait_send()


def on_device(couple, factors, top_reflect, wy_factor, neighbour_ids, kept_rank, merge_map):
    hbm, vmem = (pl.BlockSpec(memory_space=s) for s in (pl.ANY, pltpu.VMEM))
    v = lambda *shape: pltpu.VMEM(shape, BF16)
    return pl.pallas_call(
        kernel,
        name="merge_level",
        out_shape=jax.ShapeDtypeStruct((1, 1, K, HALF), BF16),
        in_specs=[hbm] * 7,
        out_specs=vmem,
        scratch_shapes=[
            pltpu.SMEM((NB, CL), jnp.int32), pltpu.SMEM((CL,), jnp.int32), pltpu.SMEM((NB, CL), jnp.int32),
            v(CL, NB, CW, CW), v(CL, CW, CW), v(CL, K, K), v(CL, K, CW),
            v(CL, HALF, HALF), pltpu.VMEM((CL, HALF), F32), v(2 * CL, HALF, HALF), v(2 * CL, HALF, HALF), pltpu.VMEM((2 * CL, HALF), F32),
            v(NB, CL, K, CW), v(3, CL, K, CW), v(2 * PER, K, CW),
            pltpu.VMEM((2, 8, 128), jnp.int32), pltpu.VMEM((3, 8, 128), jnp.int32), pltpu.SMEM((3, 8, 128), jnp.int32),
            pltpu.VMEM((EMPTY + 1, K, CW), F32), v(4, RING, K, CW),
            v(2, 2, 4, 16, CW), v(2, 2, 2, 16, CW), v(2, 4, 32, CW), v(2, 2, 4, 16, CW), v(2, 2, 4, 16, CW),
            v(2, 2, 8, 16, HALF), v(2, 2, 4, 16, HALF), v(2, 8, 32, HALF), v(2, 2, 8, 16, HALF), v(2, 2, 8, 16, HALF),
            v(8, 32, HALF), v(8, 32, HALF), v(7, 32, HALF), v(7, 32, HALF),
            pltpu.SemaphoreType.DMA((13,)), pltpu.SemaphoreType.DMA((SEMS,)), pltpu.SemaphoreType.DMA((SEMS,)),
        ],
        compiler_params=pltpu.CompilerParams(collective_id=0, has_side_effects=True, vmem_limit_bytes=62 << 20),
    )(couple, factors, top_reflect, wy_factor.transpose(0, 2, 1), neighbour_ids.T, kept_rank, merge_map.T)


def solution(mesh):
    own = ("sec", "own", "tile")
    in_specs = (P(own, None, None, None), P(own, None, None), P(own, None, None), P(own, None, None),
                P(own, None), P(own), P(own, None))
    return jax.shard_map(on_device, mesh=mesh, in_specs=in_specs, out_specs=P("sec", "own", None, "tile"), check_vma=False)
```

time: 49.7 us -> 47.7 us (0.960); the launches traced: 49.5 us -> 46.9 us
  Pallas kernels: 48.1 us -> 45.5 us
    pallas_call x1, Pallas kernels: 48.1 us -> 45.5 us  [on_device(): pl.pallas_call(kernel, name='merge_level', out_shape=jax.ShapeDtypeStruct...]
where the time goes in v2:
time: 47.7 us; the launch traced here: 46.9 us
  Pallas kernels  45.5 us (95%)
  local copies, waits for them, and re-layouts  1.32 us (3%)
    pallas_call x1, Pallas kernels, on_device(): pl.pallas_call(kernel, name='merge_level', out_shape=jax.ShapeDtypeStruct...  45.5 us
    unnamed x1, local copies, waits for them, and re-layouts  1.32 us

profile of v2, /device:TPU:6, one launch (start us, length us, event | category | flops | bytes accessed | tf_op | source)
XLA Modules:
  0.0 46.9 jit_solution(18330977320784561455)
XLA Ops:
  0.0 45.5 %merge_level.1 = bf16[1,1,64,128]{3,2,1,0:T(8,128)(2,1)} custom-call(bf16[8,3,256,256]{3,2,1,0:T(8,128)(2,1)} %couple.1, bf16[8,256,256]{2,1,0:T(8,128)(2,1)} %factors.1, bf16[8,64,64]{2,1,0:T(8,128)(2,1)} %reflect.1, bf16[8,64,256]{2,1,0:T(8,128)(2,1)} %bitcast.3, s32[3,8]{1,0:T(4,128)} %bitcast.4, s32[8]{0:T(128)} %rank_h.1, s32[3,8]{1,0:T(4,128)} %bitcast.5), custom_call_target="tpu_custom_call" | custom-call | tf_op jit(solution)/shard_map/merge_level/pallas_call | solution.py:391
  45.5 1.3 %copy.9 = bf16[1,1,64,128]{3,2,1,0:T(8,128)(2,1)} copy(bf16[1,1,64,128]{3,2,1,0:T(8,128)(2,1)} %merge_level.1) | data formatting | bytes 32768

commit v3 on v2

--- a/solution.py
+++ b/solution.py
@@ -29,7 +29,7 @@
 
 
 def kernel(couple, factors, reflect, wy, nid_h, rank_h, mmap_h, out,
-           nid, rank, mmap, couple_v, fac, refl_v, wy_v, pack, diag, sec_b, sec_u, sec_d, zs, zr, fw, tab_s, tab_v, tab, coarse, total,
+           nid, rank, mmap, couple_v, fac, refl_v, wy_v, pack, diag, sec_b, sec_u, sec_d, zs, zr, fw, tab_s, tab_v, tab, coarse, part_total, total,
            za3, za4, zad, zas, zat, ya3, ya4, yad, yas, yat, pa, pb, ra, rb,
            load_sem, ss, rs):
     sec, own, tile = lax.axis_index("sec"), lax.axis_index("own"), lax.axis_index("tile")
@@ -76,12 +76,143 @@
     def _():
         greet({"own": own + 1})
 
-    for d in (1, -1, 2, -2, 3, -3, 4):
+    for d in (2, -2, 1, -1):
         greet(zdev(d))
         greet(ydev(d))
 
-    for copy in ints:
+    at_end = own == OWNERS - 1
+    relay = ((own == 22) & (tile == 1)) | ((own == 6) & (tile == 0))
+    relay_dev = {"own": jnp.where(tile == 0, 22, 6), "tile": 1 - tile}
+
+    @pl.when(at_end)
+    def _():
+        greet(relay_dev)
+
+    @pl.when(relay)
+    def _():
+        greet({"own": OWNERS - 1, "tile": 1 - tile})
+
+    met = 2 + 8 + has_low.astype(jnp.int32) + has_up.astype(jnp.int32) + (at_end | relay).astype(jnp.int32)
+    early = z < RING // 2
+    late = z >= RING // 2
+
+    count = [0]
+
+    def remote(src, dst, to):
+        i = count[0]
+        count[0] += 1
+        return pltpu.make_async_remote_copy(src_ref=src, dst_ref=dst, send_sem=ss.at[i], recv_sem=rs.at[i],
+                                            device_id=to, device_id_type=MESH)
+
+    blocks, squares = [], []
+    for side, d in ((0, 1), (1, -1)):
+        at = pl.ds(side * CL, CL)
+        blocks.append(remote(fac.at[:, pl.ds(HALF, HALF), pl.ds(0, HALF)], sec_b.at[at], sdev(d)))
+        squares += [remote(pack, sec_u.at[at], sdev(d)), remote(diag, sec_d.at[at], sdev(d))]
+    sec_copies = blocks + squares
+    sq_r = lax.broadcasted_iota(jnp.int32, (HALF, HALF), 0)
+    sq_c = lax.broadcasted_iota(jnp.int32, (HALF, HALF), 1)
+
+    def open_up():
+        pl.semaphore_wait(barrier, met)
+        for copy in blocks:
+            copy.start()
+
+    def pack_up():
+        for c in range(CL):
+            lower = fac[c, pl.ds(HALF, HALF), pl.ds(HALF, HALF)].astype(F32)
+            diag[pl.ds(c, 1), :] = jnp.sum(jnp.where(sq_r == sq_c, lower, 0.0), axis=0, keepdims=True)
+            upper = fac[c, pl.ds(0, HALF), pl.ds(0, HALF)].astype(F32)
+            pack[c] = jnp.where(sq_r >= sq_c, upper, lower.T).astype(BF16)
+
+    base_sem = count[0]
+    count[0] += 3 * PARTS
+    fw_sem = count[0]
+    count[0] += 2
+    on_sem = count[0]
+    count[0] += 2
+    for copy in loads + ints:
         copy.wait()
+    r_iota = lax.broadcasted_iota(jnp.int32, (K, CW), 0)
+    c_iota = lax.broadcasted_iota(jnp.int32, (K, CW), 1)
+    eye = jnp.where(r_iota == c_iota, 1.0, 0.0)
+    low_group = jnp.where(has_low, 0, 2)
+    up_group = jnp.where(has_up, 1, 2)
+    cross_low = (z == 0) & has_low
+    cross_up = (z == RING - 1) & has_up
+    tops = []
+    for c in range(CL):
+        t = eye - dot(refl_v[c], wy_v[c])
+        t = jnp.where(r_iota < rank[c], t, 0.0).astype(BF16)
+        tops.append(dot(t, fac[c]).astype(BF16))
+    plain, by_way, by_relay = {}, {}, {}
+    for part in range(PARTS):
+        at = pl.ds(part * PER, PER)
+        for j in range(2):
+            group = (low_group, up_group)[j]
+            plain[j, part] = pltpu.make_async_remote_copy(
+                src_ref=zs.at[j, at], dst_ref=zr.at[group, at], send_sem=ss.at[base_sem + j * PARTS + part],
+                recv_sem=rs.at[base_sem + group * PARTS + part], device_id={"own": (low, up)[j]}, device_id_type=MESH)
+            if part < 2:
+                by_way[j, part] = pltpu.make_async_remote_copy(
+                    src_ref=zs.at[j, at], dst_ref=fw.at[at], send_sem=ss.at[base_sem + j * PARTS + part],
+                    recv_sem=rs.at[fw_sem + part], device_id=zdev((-1, 1)[j]), device_id_type=MESH)
+        if part < 2:
+            by_relay[part] = pltpu.make_async_remote_copy(
+                src_ref=zs.at[1, at], dst_ref=fw.at[at], send_sem=ss.at[base_sem + PARTS + part],
+                recv_sem=rs.at[fw_sem + part], device_id=relay_dev, device_id_type=MESH)
+
+    def z_send(part):
+        for j in (1, 0):
+            if part >= 2:
+                plain[j, part].start()
+                continue
+            crossing = (cross_low, cross_up)[j]
+
+            @pl.when(crossing)
+            def _():
+                by_way[j, part].start()
+
+            if j == 1:
+                @pl.when(at_end)
+                def _():
+                    by_relay[part].start()
+
+                crossing = crossing | at_end
+
+            @pl.when(jnp.logical_not(crossing))
+            def _():
+                plain[j, part].start()
+
+    @pl.when(early)
+    def _():
+        pack_up()
+
+    for part in range(PARTS):
+        couples[part].wait()
+        for j in (1, 0, 2):
+            for c in range(part * PER, part * PER + PER):
+                zs[j, c] = dot(tops[c], couple_v[c, j]).astype(BF16)
+
+        @pl.when(late)
+        def _():
+            if part == 0:
+                open_up()
+            z_send(part)
+
+    @pl.when(early)
+    def _():
+        open_up()
+        for part in range(PARTS):
+            z_send(part)
+
+    @pl.when(late)
+    def _():
+        pack_up()
+
+    for copy in squares:
+        copy.start()
+
     lane = lax.broadcasted_iota(jnp.int32, (8, 128), 1)
     row = lax.broadcasted_iota(jnp.int32, (8, 128), 0)
 
@@ -115,35 +246,6 @@
         tab_v[1] = nothing
 
     coarse[EMPTY] = jnp.zeros((K, CW), F32)
-    edges = has_low.astype(jnp.int32) + has_up.astype(jnp.int32)
-    pl.semaphore_wait(barrier, 2 + 14 + edges)
-
-    count = [0]
-
-    def remote(src, dst, to):
-        i = count[0]
-        count[0] += 1
-        return pltpu.make_async_remote_copy(src_ref=src, dst_ref=dst, send_sem=ss.at[i], recv_sem=rs.at[i],
-                                            device_id=to, device_id_type=MESH)
-
-    loads[0].wait()
-    sec_copies = []
-    for side, d in ((0, 1), (1, -1)):
-        copy = remote(fac.at[:, pl.ds(HALF, HALF), pl.ds(0, HALF)], sec_b.at[pl.ds(side * CL, CL)], sdev(d))
-        copy.start()
-        sec_copies.append(copy)
-    sq_r = lax.broadcasted_iota(jnp.int32, (HALF, HALF), 0)
-    sq_c = lax.broadcasted_iota(jnp.int32, (HALF, HALF), 1)
-    for c in range(CL):
-        lower = fac[c, pl.ds(HALF, HALF), pl.ds(HALF, HALF)].astype(F32)
-        diag[pl.ds(c, 1), :] = jnp.sum(jnp.where(sq_r == sq_c, lower, 0.0), axis=0, keepdims=True)
-        upper = fac[c, pl.ds(0, HALF), pl.ds(0, HALF)].astype(F32)
-        pack[c] = jnp.where(sq_r >= sq_c, upper, lower.T).astype(BF16)
-    for side, d in ((0, 1), (1, -1)):
-        at = pl.ds(side * CL, CL)
-        for copy in (remote(pack, sec_u.at[at], sdev(d)), remote(diag, sec_d.at[at], sdev(d))):
-            copy.start()
-            sec_copies.append(copy)
     to_low = remote(tab_s.at[0], tab_v.at[1], {"own": low})
     to_up = remote(tab_s.at[1], tab_v.at[0], {"own": up})
 
@@ -154,60 +256,6 @@
     @pl.when(has_up)
     def _():
         to_up.start()
-
-    base_sem = count[0]
-    count[0] += 3 * PARTS
-    fw_sem = count[0]
-    count[0] += 2
-    on_sem = count[0]
-    count[0] += 2
-    for copy in loads[1:]:
-        copy.wait()
-    r_iota = lax.broadcasted_iota(jnp.int32, (K, CW), 0)
-    c_iota = lax.broadcasted_iota(jnp.int32, (K, CW), 1)
-    eye = jnp.where(r_iota == c_iota, 1.0, 0.0)
-    low_group = jnp.where(has_low, 0, 2)
-    up_group = jnp.where(has_up, 1, 2)
-    cross_low = (z == 0) & has_low
-    cross_up = (z == RING - 1) & has_up
-    tops = []
-    for c in range(CL):
-        t = eye - dot(refl_v[c], wy_v[c])
-        t = jnp.where(r_iota < rank[c], t, 0.0).astype(BF16)
-        tops.append(dot(t, fac[c]).astype(BF16))
-    z_sends = []
-
-    def z_send(j, part):
-        at = pl.ds(part * PER, PER)
-        group = (low_group, up_group)[j]
-        to = (low, up)[j]
-        crossing = (cross_low, cross_up)[j]
-        plain = pltpu.make_async_remote_copy(
-            src_ref=zs.at[j, at], dst_ref=zr.at[group, at], send_sem=ss.at[base_sem + j * PARTS + part],
-            recv_sem=rs.at[base_sem + group * PARTS + part], device_id={"own": to}, device_id_type=MESH)
-        z_sends.append(plain)
-        if part >= 2:
-            plain.start()
-            return
-        by_way = pltpu.make_async_remote_copy(
-            src_ref=zs.at[j, at], dst_ref=fw.at[pl.ds(part * PER, PER)], send_sem=ss.at[base_sem + j * PARTS + part],
-            recv_sem=rs.at[fw_sem + part], device_id=zdev((-1, 1)[j]), device_id_type=MESH)
-
-        @pl.when(crossing)
-        def _():
-            by_way.start()
-
-        @pl.when(jnp.logical_not(crossing))
-        def _():
-            plain.start()
-
-    for part in range(PARTS):
-        couples[part].wait()
-        for j in (1, 0, 2):
-            for c in range(part * PER, part * PER + PER):
-                zs[j, c] = dot(tops[c], couple_v[c, j]).astype(BF16)
-            if j < 2:
-                z_send(j, part)
 
     def send_on(group, to, part):
         at = pl.ds(part * PER, PER)
@@ -238,6 +286,13 @@
         def _():
             fw_landed(part)
             send_on(0, own - RING, part).start()
+
+        @pl.when(relay)
+        def _():
+            fw_landed(part)
+            pltpu.make_async_remote_copy(
+                src_ref=fw.at[pl.ds(part * PER, PER)], dst_ref=zr.at[2, pl.ds(part * PER, PER)], send_sem=ss.at[on_sem + part],
+                recv_sem=rs.at[base_sem + 2 * PARTS + part], device_id={"own": OWNERS - 2, "tile": 1 - tile}, device_id_type=MESH).start()
 
     @pl.when(has_low)
     def _():
@@ -275,35 +330,53 @@
     def take(group, base, side):
         for part in range(PARTS):
             landed(group, part)
-        for part in range(PARTS):
             finish(group, base, side, part)
 
-    @pl.when(has_up)
+    up_last = z >= RING - 2
+    side_first = jnp.where(up_last, 0, 1)
+    side_last = 1 - side_first
+
+    @pl.when(jnp.logical_not(up_last))
     def _():
         take(0, 8, 1)
 
-    @pl.when(has_low)
+    @pl.when(up_last)
     def _():
         take(1, 16, 0)
-
-    @pl.when(own == 1)
-    def _():
-        take(2, 24, 0)
-
-    @pl.when(own == OWNERS - 2)
-    def _():
-        take(2, 24, 1)
 
     for yh in range(4):
         def gather(zz, _):
             m = yh * RING + zz
-            acc = coarse[tab[0, 0, m]] + coarse[tab[0, 1, m]]
-            acc = acc + coarse[tab[1, 0, m]] + coarse[tab[1, 1, m]]
-            acc = acc + coarse[tab[2, 0, m]] + coarse[tab[2, 1, m]]
+            acc = coarse[tab[2, 0, m]] + coarse[tab[2, 1, m]]
+            part_total[yh, zz] = acc + coarse[tab[side_first, 0, m]] + coarse[tab[side_first, 1, m]]
+            return 0
+
+        lax.fori_loop(0, RING, gather, 0)
+
+    @pl.when(jnp.logical_not(up_last) & has_low)
+    def _():
+        take(1, 16, 0)
+
+    @pl.when(up_last & has_up)
+    def _():
+        take(0, 8, 1)
+
+    @pl.when(own == 1)
+    def _():
+        take(2, 24, 0)
+
+    @pl.when(own == OWNERS - 2)
+    def _():
+        take(2, 24, 1)
+
+    for yh in range(4):
+        def gather_last(zz, _):
+            m = yh * RING + zz
+            acc = part_total[yh, zz] + coarse[tab[side_last, 0, m]] + coarse[tab[side_last, 1, m]]
             total[yh, zz] = acc.astype(BF16)
             return 0
 
-        lax.fori_loop(0, RING, gather, 0)
+        lax.fori_loop(0, RING, gather_last, 0)
 
     def zpiece(d, half=None, part=None):
         rows = pl.ds(0, 32) if half is None else pl.ds(16 * half, 16)
@@ -343,10 +416,13 @@
             to[far] = (mine[far].astype(F32) + third[far].astype(F32)).astype(BF16)
             twos[half, a, side] = remote(to, bs.at[half, side], dev(2 * s))
             twos[half, a, side].start()
-    for copy in list(ones.values()) + list(twos.values()):
-        copy.wait_recv()
-    sums = []
-    for piece, _, _, _, bd, bs, _, _ in axes:
+    last = []
+    for a in (1, 0):
+        piece, _, _, _, bd, bs, _, _ = axes[a]
+        for side in range(2):
+            ones[a, side].wait_recv()
+            for half in range(2):
+                twos[half, a, side].wait_recv()
         halves = []
         for half in range(2):
             rows = pl.ds(16 * half, 16)
@@ -354,19 +430,20 @@
             for side in range(2):
                 acc = acc + bd[side, :, rows, :].astype(F32) + bs[half, side].astype(F32)
             halves.append(acc)
-        sums.append(jnp.concatenate(halves, axis=1))
-    sum_a, sum_b = sums
-    for part in range(2):
-        for yh in range(4):
-            pa[2 * yh + part] = sum_a[yh, :, part * HALF:(part + 1) * HALF].astype(BF16)
-    pb[...] = sum_b.astype(BF16)
-
-    last = []
-    for d in (4, 3, 5, 2, 6, 1, 7):
-        last.append(remote(pa.at[lax.rem(y + d, RING)], ra.at[d - 1], ydev(d)))
-        last.append(remote(pb.at[lax.rem(z + d, RING)], rb.at[d - 1], zdev(d)))
-    for copy in last:
-        copy.start()
+        done = jnp.concatenate(halves, axis=1).astype(BF16)
+        if a == 1:
+            pb[...] = done
+        else:
+            for part in range(2):
+                for yh in range(4):
+                    pa[2 * yh + part] = done[yh, :, part * HALF:(part + 1) * HALF]
+        for d in (4, 3, 5, 2, 6, 1, 7):
+            if a == 1:
+                copy = remote(pb.at[lax.rem(z + d, RING)], rb.at[d - 1], zdev(d))
+            else:
+                copy = remote(pa.at[lax.rem(y + d, RING)], ra.at[d - 1], ydev(d))
+            copy.start()
+            last.append(copy)
     for copy in last:
         copy.wait_recv()
     done_a, done_b = pa[y].astype(F32), pb[z].astype(F32)
@@ -376,10 +453,10 @@
     out[0, 0, pl.ds(0, 32), :] = done_a.astype(BF16)
     out[0, 0, pl.ds(32, 32), :] = done_b.astype(BF16)
     late = [threes[0, a, side] for a, side, _ in ways]
-    for copy in z_sends + list(fours.values()) + late + list(ones.values()) + list(twos.values()) + last:
+    for copy in list(plain.values()) + list(fours.values()) + late + list(ones.values()) + list(twos.values()) + last:
         copy.wait_send()
 
-    @pl.when(on_up | on_low)
+    @pl.when(on_up | on_low | relay)
     def _():
         for part in range(2):
             send_on(1, low, part).wait_send()
@@ -400,7 +477,7 @@
             v(CL, HALF, HALF), pltpu.VMEM((CL, HALF), F32), v(2 * CL, HALF, HALF), v(2 * CL, HALF, HALF), pltpu.VMEM((2 * CL, HALF), F32),
             v(NB, CL, K, CW), v(3, CL, K, CW), v(2 * PER, K, CW),
             pltpu.VMEM((2, 8, 128), jnp.int32), pltpu.VMEM((3, 8, 128), jnp.int32), pltpu.SMEM((3, 8, 128), jnp.int32),
-            pltpu.VMEM((EMPTY + 1, K, CW), F32), v(4, RING, K, CW),
+            pltpu.VMEM((EMPTY + 1, K, CW), F32), pltpu.VMEM((4, RING, K, CW), F32), v(4, RING, K, CW),
             v(2, 2, 4, 16, CW), v(2, 2, 2, 16, CW), v(2, 4, 32, CW), v(2, 2, 4, 16, CW), v(2, 2, 4, 16, CW),
             v(2, 2, 8, 16, HALF), v(2, 2, 4, 16, HALF), v(2, 8, 32, HALF), v(2, 2, 8, 16, HALF), v(2, 2, 8, 16, HALF),
             v(8, 32, HALF), v(8, 32, HALF), v(7, 32, HALF), v(7, 32, HALF),

time: 47.7 us -> 45.8 us (0.960)
  Pallas kernels: 45.5 us -> 43.6 us
    pallas_call x1, Pallas kernels: 45.5 us -> 43.6 us  [on_device(): pl.pallas_call(kernel, name='merge_level', out_shape=jax.ShapeDtypeStruct...]
where the time goes in v3:
time: 45.8 us; the launch traced here: 45 us
  Pallas kernels  43.6 us (95%)
  local copies, waits for them, and re-layouts  1.32 us (3%)
    pallas_call x1, Pallas kernels, on_device(): pl.pallas_call(kernel, name='merge_level', out_shape=jax.ShapeDtypeStruct...  43.6 us
    unnamed x1, local copies, waits for them, and re-layouts  1.32 us

profile of v3, /device:TPU:6, one launch (start us, length us, event | category | flops | bytes accessed | tf_op | source)
XLA Modules:
  0.0 45.0 jit_solution(18155544251958496864)
XLA Ops:
  0.0 43.6 %merge_level.1 = bf16[1,1,64,128]{3,2,1,0:T(8,128)(2,1)} custom-call(bf16[8,3,256,256]{3,2,1,0:T(8,128)(2,1)} %couple.1, bf16[8,256,256]{2,1,0:T(8,128)(2,1)} %factors.1, bf16[8,64,64]{2,1,0:T(8,128)(2,1)} %reflect.1, bf16[8,64,256]{2,1,0:T(8,128)(2,1)} %bitcast.3, s32[3,8]{1,0:T(4,128)} %bitcast.4, s32[8]{0:T(128)} %rank_h.1, s32[3,8]{1,0:T(4,128)} %bitcast.5), custom_call_target="tpu_custom_call" | custom-call | tf_op jit(solution)/shard_map/merge_level/pallas_call | solution.py:468
  43.6 1.3 %copy.9 = bf16[1,1,64,128]{3,2,1,0:T(8,128)(2,1)} copy(bf16[1,1,64,128]{3,2,1,0:T(8,128)(2,1)} %merge_level.1) | data formatting | bytes 32768

commit v4 on v3

--- a/solution.py
+++ b/solution.py
@@ -80,19 +80,23 @@
         greet(zdev(d))
         greet(ydev(d))
 
+    at_start = own == 0
     at_end = own == OWNERS - 1
-    relay = ((own == 22) & (tile == 1)) | ((own == 6) & (tile == 0))
-    relay_dev = {"own": jnp.where(tile == 0, 22, 6), "tile": 1 - tile}
-
-    @pl.when(at_end)
+    for_start = ((own == 25) & (tile == 1)) | ((own == 9) & (tile == 0))
+    relay = ((own == 22) & (tile == 1)) | ((own == 6) & (tile == 0)) | for_start
+    relay_dev = {"own": jnp.where(at_start, jnp.where(tile == 0, 25, 9), jnp.where(tile == 0, 22, 6)), "tile": 1 - tile}
+    relay_from = jnp.where(for_start, 0, OWNERS - 1)
+    relay_to = jnp.where(for_start, 1, OWNERS - 2)
+
+    @pl.when(at_start | at_end)
     def _():
         greet(relay_dev)
 
     @pl.when(relay)
     def _():
-        greet({"own": OWNERS - 1, "tile": 1 - tile})
-
-    met = 2 + 8 + has_low.astype(jnp.int32) + has_up.astype(jnp.int32) + (at_end | relay).astype(jnp.int32)
+        greet({"own": relay_from, "tile": 1 - tile})
+
+    met = 2 + 8 + has_low.astype(jnp.int32) + has_up.astype(jnp.int32) + (at_start | at_end | relay).astype(jnp.int32)
     early = z < RING // 2
     late = z >= RING // 2
 
@@ -157,10 +161,9 @@
                 by_way[j, part] = pltpu.make_async_remote_copy(
                     src_ref=zs.at[j, at], dst_ref=fw.at[at], send_sem=ss.at[base_sem + j * PARTS + part],
                     recv_sem=rs.at[fw_sem + part], device_id=zdev((-1, 1)[j]), device_id_type=MESH)
-        if part < 2:
-            by_relay[part] = pltpu.make_async_remote_copy(
-                src_ref=zs.at[1, at], dst_ref=fw.at[at], send_sem=ss.at[base_sem + PARTS + part],
-                recv_sem=rs.at[fw_sem + part], device_id=relay_dev, device_id_type=MESH)
+                by_relay[j, part] = pltpu.make_async_remote_copy(
+                    src_ref=zs.at[j, at], dst_ref=fw.at[at], send_sem=ss.at[base_sem + j * PARTS + part],
+                    recv_sem=rs.at[fw_sem + part], device_id=relay_dev, device_id_type=MESH)
 
     def z_send(part):
         for j in (1, 0):
@@ -173,45 +176,17 @@
             def _():
                 by_way[j, part].start()
 
-            if j == 1:
-                @pl.when(at_end)
-                def _():
-                    by_relay[part].start()
-
-                crossing = crossing | at_end
+            doubled = (at_start, at_end)[j]
+
+            @pl.when(doubled)
+            def _():
+                by_relay[j, part].start()
+
+            crossing = crossing | doubled
 
             @pl.when(jnp.logical_not(crossing))
             def _():
                 plain[j, part].start()
-
-    @pl.when(early)
-    def _():
-        pack_up()
-
-    for part in range(PARTS):
-        couples[part].wait()
-        for j in (1, 0, 2):
-            for c in range(part * PER, part * PER + PER):
-                zs[j, c] = dot(tops[c], couple_v[c, j]).astype(BF16)
-
-        @pl.when(late)
-        def _():
-            if part == 0:
-                open_up()
-            z_send(part)
-
-    @pl.when(early)
-    def _():
-        open_up()
-        for part in range(PARTS):
-            z_send(part)
-
-    @pl.when(late)
-    def _():
-        pack_up()
-
-    for copy in squares:
-        copy.start()
 
     lane = lax.broadcasted_iota(jnp.int32, (8, 128), 1)
     row = lax.broadcasted_iota(jnp.int32, (8, 128), 0)
@@ -232,30 +207,66 @@
 
     at_low_end = jnp.full((8, 128), own, jnp.int32) == 0
     at_up_end = jnp.full((8, 128), own, jnp.int32) == OWNERS - 1
-    tab_s[0] = table([(0, 8, None), (1, 24, at_up_end)])
-    tab_s[1] = table([(1, 16, None), (0, 24, at_low_end)])
-    tab_v[2] = table([(2, 0, None)])
-    nothing = jnp.where(row < 2, EMPTY, 0)
-
-    @pl.when(jnp.logical_not(has_low))
-    def _():
-        tab_v[0] = nothing
-
-    @pl.when(jnp.logical_not(has_up))
-    def _():
-        tab_v[1] = nothing
-
-    coarse[EMPTY] = jnp.zeros((K, CW), F32)
     to_low = remote(tab_s.at[0], tab_v.at[1], {"own": low})
     to_up = remote(tab_s.at[1], tab_v.at[0], {"own": up})
 
-    @pl.when(has_low)
-    def _():
-        to_low.start()
-
-    @pl.when(has_up)
-    def _():
-        to_up.start()
+    def fill_tables():
+        tab_s[0] = table([(0, 8, None), (1, 24, at_up_end)])
+        tab_s[1] = table([(1, 16, None), (0, 24, at_low_end)])
+        tab_v[2] = table([(2, 0, None)])
+        nothing = jnp.where(row < 2, EMPTY, 0)
+
+        @pl.when(jnp.logical_not(has_low))
+        def _():
+            tab_v[0] = nothing
+
+        @pl.when(jnp.logical_not(has_up))
+        def _():
+            tab_v[1] = nothing
+
+        coarse[EMPTY] = jnp.zeros((K, CW), F32)
+
+    def send_tables():
+        @pl.when(has_low)
+        def _():
+            to_low.start()
+
+        @pl.when(has_up)
+        def _():
+            to_up.start()
+
+    @pl.when(early)
+    def _():
+        fill_tables()
+        pack_up()
+
+    for part in range(PARTS):
+        couples[part].wait()
+        for j in (1, 0, 2):
+            for c in range(part * PER, part * PER + PER):
+                zs[j, c] = dot(tops[c], couple_v[c, j]).astype(BF16)
+
+        @pl.when(late)
+        def _():
+            if part == 0:
+                open_up()
+            z_send(part)
+
+    @pl.when(early)
+    def _():
+        open_up()
+        for part in range(PARTS):
+            z_send(part)
+        send_tables()
+
+    @pl.when(late)
+    def _():
+        fill_tables()
+        send_tables()
+        pack_up()
+
+    for copy in squares:
+        copy.start()
 
     def send_on(group, to, part):
         at = pl.ds(part * PER, PER)
@@ -292,7 +303,7 @@
             fw_landed(part)
             pltpu.make_async_remote_copy(
                 src_ref=fw.at[pl.ds(part * PER, PER)], dst_ref=zr.at[2, pl.ds(part * PER, PER)], send_sem=ss.at[on_sem + part],
-                recv_sem=rs.at[base_sem + 2 * PARTS + part], device_id={"own": OWNERS - 2, "tile": 1 - tile}, device_id_type=MESH).start()
+                recv_sem=rs.at[base_sem + 2 * PARTS + part], device_id={"own": relay_to, "tile": 1 - tile}, device_id_type=MESH).start()
 
     @pl.when(has_low)
     def _():
@@ -330,6 +341,7 @@
     def take(group, base, side):
         for part in range(PARTS):
             landed(group, part)
+        for part in range(PARTS):
             finish(group, base, side, part)
 
     up_last = z >= RING - 2

time: 45.8 us -> 44.6 us (0.974)
  Pallas kernels: 43.6 us -> 42.8 us
    pallas_call x1, Pallas kernels: 43.6 us -> 42.8 us  [on_device(): pl.pallas_call(kernel, name='merge_level', out_shape=jax.ShapeDtypeStruct...]
where the time goes in v4:
time: 44.6 us; the launch traced here: 44.1 us
  Pallas kernels  42.8 us (96%)
  local copies, waits for them, and re-layouts  1.32 us (3%)
    pallas_call x1, Pallas kernels, on_device(): pl.pallas_call(kernel, name='merge_level', out_shape=jax.ShapeDtypeStruct...  42.8 us
    unnamed x1, local copies, waits for them, and re-layouts  1.32 us

profile of v4, /device:TPU:6, one launch (start us, length us, event | category | flops | bytes accessed | tf_op | source)
XLA Modules:
  0.0 44.1 jit_solution(6850554684807502581)
XLA Ops:
  0.0 42.8 %merge_level.1 = bf16[1,1,64,128]{3,2,1,0:T(8,128)(2,1)} custom-call(bf16[8,3,256,256]{3,2,1,0:T(8,128)(2,1)} %couple.1, bf16[8,256,256]{2,1,0:T(8,128)(2,1)} %factors.1, bf16[8,64,64]{2,1,0:T(8,128)(2,1)} %reflect.1, bf16[8,64,256]{2,1,0:T(8,128)(2,1)} %bitcast.3, s32[3,8]{1,0:T(4,128)} %bitcast.4, s32[8]{0:T(128)} %rank_h.1, s32[3,8]{1,0:T(4,128)} %bitcast.5), custom_call_target="tpu_custom_call" | custom-call | tf_op jit(solution)/shard_map/merge_level/pallas_call | solution.py:480
  42.8 1.3 %copy.9 = bf16[1,1,64,128]{3,2,1,0:T(8,128)(2,1)} copy(bf16[1,1,64,128]{3,2,1,0:T(8,128)(2,1)} %merge_level.1) | data formatting | bytes 32768

commit v5 on v4

--- a/solution.py
+++ b/solution.py
@@ -402,7 +402,7 @@
         return total.at[to // 2, which, rows, pl.ds(pl.multiple_of(lax.rem(to, 2) * HALF, HALF), HALF)]
 
     axes = ((zpiece, zdev, za3, za4, zad, zas, zat, 2), (ypiece, ydev, ya3, ya4, yad, yas, yat, 4))
-    ways = [(a, side, s) for a in range(2) for side, s in ((0, 1), (1, -1))]
+    ways = [(a, side, s) for a in (1, 0) for side, s in ((0, 1), (1, -1))]
     fours, threes, ones, twos = {}, {}, {}, {}
     for half in range(2):
         for a, side, s in ways:

time: 44.6 us -> 44.5 us (level)
  no operation moved by 1% of the time
where the time goes in v5:
time: 44.5 us; the launch traced here: 44.1 us
  Pallas kernels  42.7 us (96%)
  local copies, waits for them, and re-layouts  1.32 us (3%)
    pallas_call x1, Pallas kernels, on_device(): pl.pallas_call(kernel, name='merge_level', out_shape=jax.ShapeDtypeStruct...  42.7 us
    unnamed x1, local copies, waits for them, and re-layouts  1.32 us

profile of v5, /device:TPU:6, one launch (start us, length us, event | category | flops | bytes accessed | tf_op | source)
XLA Modules:
  0.0 44.1 jit_solution(9731041386120172986)
XLA Ops:
  0.0 42.7 %merge_level.1 = bf16[1,1,64,128]{3,2,1,0:T(8,128)(2,1)} custom-call(bf16[8,3,256,256]{3,2,1,0:T(8,128)(2,1)} %couple.1, bf16[8,256,256]{2,1,0:T(8,128)(2,1)} %factors.1, bf16[8,64,64]{2,1,0:T(8,128)(2,1)} %reflect.1, bf16[8,64,256]{2,1,0:T(8,128)(2,1)} %bitcast.3, s32[3,8]{1,0:T(4,128)} %bitcast.4, s32[8]{0:T(128)} %rank_h.1, s32[3,8]{1,0:T(4,128)} %bitcast.5), custom_call_target="tpu_custom_call" | custom-call | tf_op jit(solution)/shard_map/merge_level/pallas_call | solution.py:480
  42.8 1.3 %copy.9 = bf16[1,1,64,128]{3,2,1,0:T(8,128)(2,1)} copy(bf16[1,1,64,128]{3,2,1,0:T(8,128)(2,1)} %merge_level.1) | data formatting | bytes 32768
